TPU v7x, 32 devices: a whole 2x2x4 slice. The times are simulated.
32 devices in a mesh: groups: 2 (over x), docs: 16 (over z, y, core).
Axes of the slice: x: 2, y: 2, z: 4, core: 2. Of those that a mesh axis runs over, the one named last changes fastest.
Arguments:
- doc_acts: bfloat16 [2, 4096, 4096], P(None, ('groups', 'docs')), parts along dimension 1, may hold values from -6 to 6
- doc_grads: bfloat16 [2, 4096, 11008], P(None, ('groups', 'docs')), parts along dimension 1, may hold values from -6 to 6
- doc_segments: int32 [32, 128], P(('groups', 'docs')), parts along dimension 0, may hold values from 0 to 15, never falling along the last dimension, each value on 1 to 16 neighbouring positions
- query_acts: bfloat16 [2, 2048, 4096], P(None, ('groups', 'docs')), parts along dimension 1, may hold values from -6 to 6
- query_grads: bfloat16 [2, 2048, 11008], P(None, ('groups', 'docs')), parts along dimension 1, may hold values from -6 to 6
- query_segments: int32 [32, 64], P(('groups', 'docs')), parts along dimension 0, may hold values from 0 to 3, never falling along the last dimension, each value on 1 to 24 neighbouring positions
- input_proj: bfloat16 [4096, 64], replicated, may hold values from -0.09375 to 0.09375
- output_proj: bfloat16 [11008, 64], replicated, may hold values from -0.0546875 to 0.0546875
- step_rates: float32 [2], replicated, may hold values from 0.5 to 2
Outputs:
- scores: float32 [512, 64], P(('groups', 'docs')), parts along dimension 0
There are 2 independent parts, one for each index of `groups`. A program takes and returns all parts, laid end to end along the dimension named above; an argument that names none is the same for every part. Nothing has to cross between parts.
Inputs may be any that keep to these rules, and one draw needn't show every extreme that they name: `doc_segments`: within each row the numbers never fall; each of the 16 documents of a row has 1 to 16 tokens, and some document has 16. `query_segments`: within each row the numbers never fall; each of the 4 queries of a row has 1 to 24 tokens, and some query has 24.
All inputs are finite; a program needn't handle non-finite values.
Results may differ from a plain program's by a relative error of at most 0.0065.
Values may be sent and summed in bfloat16 or wider, within the bound.
A program may use at most 128 MiB of HBM per device.

v0:
```python
import jax
import jax.numpy as jnp
from jax import lax
from jax.sharding import PartitionSpec as P

DOCS_DEV = 16
Q_DEV = 4


def project_tokens(activ, gradient, input_proj, output_proj):
    left_proj = jnp.dot(activ, input_proj, preferred_element_type=jnp.float32).astype(jnp.bfloat16)
    right_proj = jnp.dot(gradient, output_proj, preferred_element_type=jnp.float32).astype(
        jnp.bfloat16
    )
    return (left_proj, right_proj)


def fold_features(left_proj, right_proj, segment_row, count):
    width = left_proj.shape[1]
    onehot = (segment_row[:, None] == jnp.arange(count, dtype=jnp.int32)[None, :]).astype(
        jnp.bfloat16
    )
    spread = (onehot[:, :, None] * left_proj[:, None, :]).reshape(left_proj.shape[0], count * width)
    summed = lax.dot_general(
        spread, right_proj, (((0,), (0,)), ((), ())), preferred_element_type=jnp.float32
    )
    return summed.reshape(count, width * width)


def doc_blocks(doc_acts, doc_grads, doc_segments, input_proj, output_proj, step_rates):
    result = []
    for checkpoint in range(doc_acts.shape[0]):
        left_proj, right_proj = project_tokens(
            doc_acts[checkpoint], doc_grads[checkpoint], input_proj, output_proj
        )
        block = fold_features(left_proj, right_proj, doc_segments[0], DOCS_DEV)
        result.append((block * step_rates[checkpoint]).astype(jnp.bfloat16))
    return result


def query_projections(query_acts, query_grads, input_proj, output_proj):
    lefts = []
    rights = []
    for checkpoint in range(query_acts.shape[0]):
        left_proj, right_proj = project_tokens(
            query_acts[checkpoint], query_grads[checkpoint], input_proj, output_proj
        )
        lefts.append(left_proj)
        rights.append(right_proj)
    return (lefts, rights)


def place_block(doc_feat, piece):
    part_scores = lax.dot_general(
        doc_feat.astype(jnp.float32),
        piece,
        (((1,), (1,)), ((), ())),
        precision=lax.Precision.HIGHEST,
        preferred_element_type=jnp.float32,
    )
    return part_scores


def per_device(
    doc_acts,
    doc_grads,
    doc_segments,
    query_acts,
    query_grads,
    query_segments,
    input_proj,
    output_proj,
    step_rates,
):
    width = input_proj.shape[1]
    total_queries = Q_DEV * lax.axis_size("docs")
    lefts, rights = query_projections(query_acts, query_grads, input_proj, output_proj)
    query_list = [
        fold_features(lefts[c], rights[c], query_segments[0], Q_DEV) for c in range(len(lefts))
    ]
    doc_list = doc_blocks(doc_acts, doc_grads, doc_segments, input_proj, output_proj, step_rates)
    total = jnp.zeros((DOCS_DEV, total_queries), jnp.float32)
    for checkpoint in range(len(doc_list)):
        partial_scores = place_block(
            doc_list[checkpoint], lax.all_gather(query_list[checkpoint], "docs", axis=0, tiled=True)
        )
        total = total + partial_scores
    return total * (4.0 / (width * width))


def solution(mesh):
    return jax.shard_map(
        per_device,
        mesh=mesh,
        in_specs=(
            P(None, ("groups", "docs"), None),
            P(None, ("groups", "docs"), None),
            P(("groups", "docs"), None),
            P(None, ("groups", "docs"), None),
            P(None, ("groups", "docs"), None),
            P(("groups", "docs"), None),
            P(),
            P(),
            P(),
        ),
        out_specs=P(("groups", "docs"), None),
        check_vma=False,
    )
```

profile of v0, /device:TPU:0, one launch (start us, length us, event | category | flops | bytes accessed | tf_op | source)
XLA Modules:
  0.0 102.3 jit_solution(9605816437802377426)
XLA Ops:
  6.5 0.0 copy-start
  6.5 0.0 copy-start.2
  6.5 0.0 all-gather.5.cloned.1.call-start
  6.5 1.6 %convolution_convert_fusion.2 = bf16[64,64]{1,0:T(8,128)(2,1)S(1)} fusion(bf16[4096,64]{0,1:T(8,128)(2,1)} %param.15, bf16[2,64,4096]{2,1,0:T(8,128)(2,1)} %param.12), kind=kOutput, calls=%fused_computation.22 | convolution fusion | flops 33558528 | bytes 1056768 | tf_op jit(solution)/shard_map/dot_general | solution.py:11
  8.2 1.5 %convolution_convert_fusion.3 = bf16[64,64]{1,0:T(8,128)(2,1)S(1)} fusion(bf16[4096,64]{0,1:T(8,128)(2,1)} %param.15, bf16[2,64,4096]{2,1,0:T(8,128)(2,1)} %param.12), kind=kOutput, calls=%fused_computation.23 | convolution fusion | flops 33558528 | bytes 1056768 | tf_op jit(solution)/shard_map/dot_general | solution.py:11
  9.6 0.0 copy-done.2
  9.7 0.1 fusion.45
  9.7 0.1 broadcast_multiply_fusion.2
  9.9 0.1 mul.93
  10.0 0.0 copy-done
  10.0 2.0 %fusion.34 = f32[256,64]{1,0:T(8,128)S(1)} fusion(bf16[64,256]{1,0:T(8,128)(2,1)S(1)} %mul.93, bf16[11008,64]{0,1:T(8,128)(2,1)S(1)} %copy-done, bf16[2,64,11008]{2,1,0:T(8,128)(2,1)} %param.13), kind=kOutput, calls=%fused_computation.25 | convolution fusion | flops 92278784 | bytes 2916352 | tf_op jit(solution)/shard_map/dot_general | solution.py:24
  12.0 0.0 copy-start.1
  12.0 0.0 copy-start.3
  12.0 0.0 copy-start.4
  12.1 0.7 reshape.86
  12.8 0.0 all-gather.5.cloned.1.call-update
  12.8 0.0 all-gather.7.cloned.1.call-start
  12.9 0.1 mul.101
  13.0 2.0 %fusion.31 = f32[256,64]{1,0:T(8,128)S(1)} fusion(bf16[64,256]{1,0:T(8,128)(2,1)S(1)} %mul.101, bf16[11008,64]{0,1:T(8,128)(2,1)S(1)} %copy-done, bf16[2,64,11008]{2,1,0:T(8,128)(2,1)} %param.13), kind=kOutput, calls=%fused_computation.24 | convolution fusion | flops 92278784 | bytes 2916352 | tf_op jit(solution)/shard_map/dot_general | solution.py:24
  15.0 0.7 reshape.88
  15.7 0.0 all-gather.7.cloned.1.call-update
  15.8 0.0 copy-done.1
  15.8 0.6 fusion.47
  16.4 0.0 copy-done.3
  16.4 0.0 copy-done.4
  16.4 1.7 %convolution_convert_fusion = bf16[128,64]{0,1:T(8,128)(2,1)S(1)} fusion(bf16[4096,64]{0,1:T(8,128)(2,1)S(1)} %copy-done.4, bf16[2,128,4096]{2,1,0:T(8,128)(2,1)} %param.9), kind=kOutput, calls=%fused_computation.16 | convolution fusion | flops 67117056 | bytes 1589248 | tf_op jit(solution)/shard_map/dot_general | solution.py:11
  18.1 1.7 %convolution_convert_fusion.1 = bf16[128,64]{0,1:T(8,128)(2,1)S(1)} fusion(bf16[4096,64]{0,1:T(8,128)(2,1)S(1)} %copy-done.4, bf16[2,128,4096]{2,1,0:T(8,128)(2,1)} %param.9), kind=kOutput, calls=%fused_computation.17 | convolution fusion | flops 67117056 | bytes 1589248 | tf_op jit(solution)/shard_map/dot_general | solution.py:11
  19.9 3.8 %fusion.12 = bf16[1024,64]{0,1:T(8,128)(2,1)S(1)} fusion(bf16[128,1024]{0,1:T(8,128)(2,1)S(1)} %bitcast.63, bf16[11008,64]{0,1:T(8,128)(2,1)S(1)} %copy-done, bf16[2,128,11008]{2,1,0:T(8,128)(2,1)} %param.10, f32[]{:T(128)} %bitcast.4), kind=kOutput, calls=%fused_computation.14 | convolution fusion | flops 197271552 | bytes 4620800 | tf_op jit(solution)/shard_map/dot_general | solution.py:24
  23.7 0.2 copy.16
  23.8 0.3 convert_element_type.58
  24.1 3.8 %fusion.13 = bf16[1024,64]{0,1:T(8,128)(2,1)S(1)} fusion(bf16[128,1024]{0,1:T(8,128)(2,1)S(1)} %bitcast.62, bf16[11008,64]{0,1:T(8,128)(2,1)S(1)} %copy-done, bf16[2,128,11008]{2,1,0:T(8,128)(2,1)} %param.10, f32[]{:T(128)} %bitcast.11), kind=kOutput, calls=%fused_computation.15 | convolution fusion | flops 197271552 | bytes 4620800 | tf_op jit(solution)/shard_map/dot_general | solution.py:24
  27.9 0.2 copy.18
  28.1 0.3 convert_element_type.65
  28.4 25.2 %all-gather.5.cloned.1.call-done = f32[16,4,4096]{2,1,0:T(4,128)} async-done(((f32[1,4,4096]{2,1,0:T(4,128)}), f32[16,4,4096]{2,1,0:T(4,128)}) %all-gather.5.cloned.1.call-update) | async-done | bytes 1048592 | tf_op jit(solution)/shard_map/all_gather | solution.py:85
  53.6 1.6 %reshape.87 = f32[64,4096]{1,0:T(8,128)S(1)} reshape(f32[16,4,4096]{2,1,0:T(4,128)} %all-gather.5.cloned.1.call-done) | data formatting | bytes 2097152
  55.2 0.6 fusion.48
  55.8 36.9 %all-gather.7.cloned.1.call-done = f32[16,4,4096]{2,1,0:T(4,128)} async-done(((f32[1,4,4096]{2,1,0:T(4,128)}), f32[16,4,4096]{2,1,0:T(4,128)}) %all-gather.7.cloned.1.call-update) | async-done | bytes 1048592 | tf_op jit(solution)/shard_map/all_gather | solution.py:85
  92.7 1.6 %reshape.89 = f32[64,4096]{1,0:T(8,128)S(1)} reshape(f32[16,4,4096]{2,1,0:T(4,128)} %all-gather.7.cloned.1.call-done) | data formatting | bytes 2097152
  94.3 1.2 %fusion.36 = f32[16,64]{1,0:T(8,128)} fusion(f32[16,64]{1,0:T(8,128)S(1)} %fusion.48, bf16[16,4096]{1,0:T(8,128)(2,1)S(1)} %convert_element_type.65, f32[64,4096]{1,0:T(8,128)S(1)} %reshape.89), kind=kOutput, calls=%fused_computation.27 | convolution fusion | flops 50333696 | bytes 1187840 | tf_op jit(solution)/shard_map/dot_general | solution.py:54
  (2 shorter events, 0.0 us)
Async XLA Ops:
  6.5 3.5 %copy-start = (bf16[11008,64]{0,1:T(8,128)(2,1)S(1)}, bf16[11008,64]{0,1:T(8,128)(2,1)}, u32[]{:S(2)}) copy-start(bf16[11008,64]{0,1:T(8,128)(2,1)} %param.16) | copy-start | bytes 4227076
  6.5 3.1 %copy-start.2 = (s32[1,64]{1,0:T(1,128)S(1)}, s32[1,64]{1,0:T(1,128)}, u32[]{:S(2)}) copy-start(s32[1,64]{1,0:T(1,128)} %param.14) | copy-start | bytes 772
  6.5 47.1 %all-gather.5.cloned.1.call-start = ((), (), s32[]{:S(2)}) async-start(), calls=%async_computation | async-start | bytes 1114112 | tf_op jit(solution)/shard_map/all_gather | solution.py:85
  12.0 3.8 %copy-start.1 = (f32[2]{0:T(128)S(1)}, f32[2]{0:T(128)}, u32[]{:S(2)}) copy-start(f32[2]{0:T(128)} %param.17) | copy-start | bytes 28
  12.0 4.3 %copy-start.3 = (s32[1,128]{1,0:T(1,128)S(1)}, s32[1,128]{1,0:T(1,128)}, u32[]{:S(2)}) copy-start(s32[1,128]{1,0:T(1,128)} %param.11) | copy-start | bytes 1540
  12.0 4.3 %copy-start.4 = (bf16[4096,64]{0,1:T(8,128)(2,1)S(1)}, bf16[4096,64]{0,1:T(8,128)(2,1)}, u32[]{:S(2)}) copy-start(bf16[4096,64]{0,1:T(8,128)(2,1)} %param.15) | copy-start | bytes 1572868
  12.8 79.8 %all-gather.7.cloned.1.call-start = ((), (), s32[]{:S(2)}) async-start(), calls=%async_computation.1 | async-start | bytes 1114112 | tf_op jit(solution)/shard_map/all_gather | solution.py:85
Sparse Core Ops, SparseCore 0:
  12.9 40.6 all-gather.4
  55.8 36.8 all-gather.6
where the time goes:
time: 103 us; the launch traced here: 102 us
  waiting for transfers between devices  62.2 us (60%)
  matrix products  19.9 us (19%)
  between operations  13.5 us (13%)
  local copies, waits for them, and re-layouts  6.36 us (6%)
    all_gather x2, waiting for transfers between devices, per_device(): lax.all_gather(query_list[checkpoint], 'docs', axis=0, tiled=True)  62.1 us
    dot_general x4, matrix products, fold_features(): lax.dot_general(spread, right_proj, (((0,), (0,)), ((), ())), preferred_e...  11.6 us
    dot_general x4, matrix products, project_tokens(): jnp.dot(activ, input_proj, preferred_element_type=jnp.float32)  6.52 us
    unnamed x14, local copies, waits for them, and re-layouts  4.66 us
  transfers between devices with their start and end apart: 2, of which 2 were waited for; matrix products, arithmetic and copies ran while one was open for 17% of the time, Pallas kernels for 0%

commit v1 on v0

v1 whole, which is shorter than its diff:
```python
import functools

import jax
import jax.numpy as jnp
from jax import lax
from jax.experimental import pallas as pl
from jax.experimental.pallas import tpu as pltpu
from jax.sharding import PartitionSpec as P

DOCS_DEV = 16
Q_DEV = 4
TAG = 16
MESH = pl.DeviceIdType.MESH
NT = (((1,), (1,)), ((), ()))


def cuts(extent, parts):
    units = extent // 256
    edges = [256 * (units * i // parts) for i in range(parts)] + [extent]
    return list(zip(edges[:-1], edges[1:]))


def flipped(value, mask):
    bit = 1
    while bit <= mask:
        if mask & bit:
            value = value + bit - 2 * bit * ((value // bit) % 2)
        bit *= 2
    return value


def kernel(
    outer,
    inner,
    act_cuts,
    grad_cuts,
    qa_hbm,
    qg_hbm,
    qs_hbm,
    da_hbm,
    dg_hbm,
    ds_hbm,
    wi_hbm,
    wo_hbm,
    rates_ref,
    out_ref,
    qa,
    qg,
    qs,
    da,
    dg,
    ds,
    wi,
    wo,
    lefts,
    rights,
    folded,
    load_sem,
    send_sem,
    recv_sem,
):
    me = lax.axis_index("docs")
    core, chip = me % 2, me // 2
    row, col = chip // inner, chip % inner
    n_pairs = outer * inner
    qtok = qs.shape[1]
    tok = ds.shape[1]

    def at(r, c, k):
        return (r * inner + c) * 2 + k

    loads = []

    def load(src, dst):
        copy = pltpu.make_async_copy(src, dst, load_sem.at[len(loads)])
        copy.start()
        loads.append(copy)
        return copy

    qs_load = load(qs_hbm, qs)
    wi_loads, qa_loads = [], []
    for a, b in act_cuts:
        wi_loads.append(load(wi_hbm.at[:, a:b], wi.at[:, a:b]))
        qa_loads.append(load(qa_hbm.at[:, :, a:b], qa.at[:, :, a:b]))
    wo_loads, qg_loads = [], []
    for a, b in grad_cuts:
        wo_loads.append(load(wo_hbm.at[:, a:b], wo.at[:, a:b]))
        qg_loads.append(load(qg_hbm.at[:, :, a:b], qg.at[:, :, a:b]))
    ds_load = load(ds_hbm, ds)
    da_loads = [load(da_hbm.at[:, :, a:b], da.at[:, :, a:b]) for a, b in act_cuts]
    dg_loads = [load(dg_hbm.at[:, :, a:b], dg.at[:, :, a:b]) for a, b in grad_cuts]

    rows_away = [flipped(row, i) for i in range(1, outer)]
    cols_away = [flipped(col, i) for i in range(1, inner)]
    peers = [at(r, col, core) for r in rows_away]
    peers += [at(row, c, core) for c in cols_away]
    peers += [at(row, col, 1 - core)]
    barrier = pltpu.get_barrier_semaphore()
    for peer in peers:
        pl.semaphore_signal(barrier, inc=1, device_id={"docs": peer}, device_id_type=MESH)

    sends = []

    def send(kind, slot, peer):
        block = (lefts, rights)[kind].at[slot]
        copy = pltpu.make_async_remote_copy(
            src_ref=block,
            dst_ref=block,
            send_sem=send_sem.at[len(sends)],
            recv_sem=recv_sem.at[kind, slot],
            device_id={"docs": peer},
            device_id_type=MESH,
        )
        copy.start()
        sends.append(copy)

    def arrived(kind, slot):
        block = (lefts, rights)[kind].at[slot]
        pltpu.make_async_remote_copy(
            src_ref=block,
            dst_ref=block,
            send_sem=send_sem.at[0],
            recv_sem=recv_sem.at[kind, slot],
            device_id={"docs": peers[-1]},
            device_id_type=MESH,
        ).wait_recv()

    def project(x, w, w_loads, x_loads, ranges):
        rows = x.shape[0] * x.shape[1]
        total = None
        for i, (a, b) in enumerate(ranges):
            if w_loads is not None:
                w_loads[i].wait()
            x_loads[i].wait()
            part = lax.dot_general(
                x[:, :, a:b].reshape(rows, b - a), w[:, a:b], NT, preferred_element_type=jnp.float32
            )
            total = part if total is None else total + part
        return total

    def beside(total):
        half = total.shape[0] // 2
        return jnp.concatenate([total[:half], total[half:]], axis=1).astype(jnp.bfloat16)

    qs_load.wait()
    width = 2 * qtok
    doubled = jnp.concatenate([qs[...], qs[...]], axis=1)
    lane = lax.broadcasted_iota(jnp.int32, (TAG, width), 1)
    line = lax.broadcasted_iota(jnp.int32, (TAG, width), 0)
    mine = (line == doubled + (me % (TAG // Q_DEV)) * Q_DEV) & (lane // qtok == core)
    lefts[me, qtok:, :] = mine.astype(jnp.float32).astype(jnp.bfloat16)
    lefts[me, :qtok, :] = beside(project(qa, wi, wi_loads, qa_loads, act_cuts))
    pl.semaphore_wait(barrier, len(peers))
    for peer in peers:
        send(0, me, peer)
    rights[me, :, :] = beside(project(qg, wo, wo_loads, qg_loads, grad_cuts))
    for peer in peers:
        send(1, me, peer)

    def pass_rows(kind):
        for r in rows_away:
            slot = at(r, col, core)
            arrived(kind, slot)
            for c in cols_away:
                send(kind, slot, at(row, c, core))
            send(kind, slot, at(row, col, 1 - core))

    def pass_cols(kind):
        for c in cols_away:
            for r in [row] + rows_away:
                slot = at(r, c, core)
                arrived(kind, slot)
                send(kind, slot, at(row, col, 1 - core))

    def spread(total):
        half = total.shape[0] // 2
        zero = jnp.zeros((half, total.shape[1]), jnp.float32)
        top = jnp.concatenate([total[:half], zero], axis=1)
        low = jnp.concatenate([zero, total[half:]], axis=1)
        return jnp.concatenate([top, low], axis=0).astype(jnp.bfloat16)

    doc_left = spread(project(da, wi, None, da_loads, act_cuts))
    pass_rows(0)
    doc_right = spread(project(dg, wo, None, dg_loads, grad_cuts))
    pass_rows(1)
    pass_cols(0)
    pass_cols(1)
    ds_load.wait()
    of_doc = lax.broadcasted_iota(jnp.int32, (DOCS_DEV, tok), 0) == ds[...]
    of_doc = of_doc.astype(jnp.float32).astype(jnp.bfloat16)
    of_doc = jnp.concatenate([of_doc, of_doc], axis=1)

    def fold(pair):
        left = lefts[pl.ds(2 * pair, 2), :qtok, :].reshape(width, -1)
        right = rights[pl.ds(2 * pair, 2), :, :].reshape(width, -1)
        a = lax.dot_general(doc_left, left, NT, preferred_element_type=jnp.float32)
        b = lax.dot_general(doc_right, right, NT, preferred_element_type=jnp.float32)
        ab = a * b
        s = ab[:tok] * rates_ref[0] + ab[tok:] * rates_ref[1]
        high = s.astype(jnp.bfloat16)
        low = (s - high.astype(jnp.float32)).astype(jnp.bfloat16)
        folded[pair] = jnp.dot(
            of_doc, jnp.concatenate([high, low], axis=0), preferred_element_type=jnp.float32
        )

    for c in [col] + cols_away:
        for r in [row] + rows_away:
            slot = at(r, c, 1 - core)
            arrived(0, slot)
            arrived(1, slot)
            fold(r * inner + c)

    chips = TAG // Q_DEV // 2
    group = min(n_pairs, 16)
    for g in range(0, n_pairs, group):
        t = jnp.concatenate([folded[p] for p in range(g, g + group)], axis=1)
        high = t.astype(jnp.bfloat16)
        low = (t - high.astype(jnp.float32)).astype(jnp.bfloat16)
        zero = jnp.zeros((TAG, width), jnp.bfloat16)
        lines = []
        for first in range(g, g + group, chips):
            lines.append(
                jnp.concatenate(
                    [
                        lefts[2 * p, qtok:, :] + lefts[2 * p + 1, qtok:, :]
                        if first <= p < first + chips
                        else zero
                        for p in range(g, g + group)
                    ],
                    axis=1,
                )
            )
        of_query = jnp.concatenate(lines, axis=0)
        both = lax.dot_general(
            jnp.concatenate([high, low], axis=0), of_query, NT, preferred_element_type=jnp.float32
        )
        k = doc_left.shape[1] // 2
        out_ref[:, g * 2 * Q_DEV : (g + group) * 2 * Q_DEV] = (both[:DOCS_DEV] + both[DOCS_DEV:]) * (
            4.0 / (k * k)
        )

    for copy in sends:
        copy.wait_send()


def per_device(
    doc_acts,
    doc_grads,
    doc_segments,
    query_acts,
    query_grads,
    query_segments,
    input_proj,
    output_proj,
    step_rates,
):
    n = lax.axis_size("docs")
    chips = n // 2
    inner = 1
    while 4 * inner * inner <= chips and chips % (2 * inner) == 0:
        inner *= 2
    outer = chips // inner
    d, k = input_proj.shape
    f = output_proj.shape[0]
    qtok = query_segments.shape[1]
    act_cuts, grad_cuts = cuts(d, 2), cuts(f, 4)
    n_loads = 2 + 3 * len(act_cuts) + 3 * len(grad_cuts)
    n_sends = 2 * (outer * inner + (outer - 1) * inner + inner - 1 + 1)
    hbm = pl.BlockSpec(memory_space=pl.ANY)
    return pl.pallas_call(
        functools.partial(kernel, outer, inner, act_cuts, grad_cuts),
        out_shape=jax.ShapeDtypeStruct((DOCS_DEV, Q_DEV * n), jnp.float32),
        in_specs=[hbm] * 8 + [pl.BlockSpec(memory_space=pltpu.SMEM)],
        out_specs=pl.BlockSpec(memory_space=pltpu.VMEM),
        scratch_shapes=[
            pltpu.VMEM(query_acts.shape, jnp.bfloat16),
            pltpu.VMEM(query_grads.shape, jnp.bfloat16),
            pltpu.VMEM(query_segments.shape, jnp.int32),
            pltpu.VMEM(doc_acts.shape, jnp.bfloat16),
            pltpu.VMEM(doc_grads.shape, jnp.bfloat16),
            pltpu.VMEM(doc_segments.shape, jnp.int32),
            pltpu.VMEM((k, d), jnp.bfloat16),
            pltpu.VMEM((k, f), jnp.bfloat16),
            pltpu.VMEM((n, qtok + TAG, 2 * k), jnp.bfloat16),
            pltpu.VMEM((n, qtok, 2 * k), jnp.bfloat16),
            pltpu.VMEM((chips, DOCS_DEV, 2 * qtok), jnp.float32),
            pltpu.SemaphoreType.DMA((n_loads,)),
            pltpu.SemaphoreType.DMA((n_sends,)),
            pltpu.SemaphoreType.DMA((2, n)),
        ],
        compiler_params=pltpu.CompilerParams(
            collective_id=0, has_side_effects=True, vmem_limit_bytes=56 << 20
        ),
    )(
        query_acts,
        query_grads,
        query_segments,
        doc_acts,
        doc_grads,
        doc_segments,
        input_proj.T,
        output_proj.T,
        step_rates,
    )


def solution(mesh):
    return jax.shard_map(
        per_device,
        mesh=mesh,
        in_specs=(
            P(None, ("groups", "docs"), None),
            P(None, ("groups", "docs"), None),
            P(("groups", "docs"), None),
            P(None, ("groups", "docs"), None),
            P(None, ("groups", "docs"), None),
            P(("groups", "docs"), None),
            P(),
            P(),
            P(),
        ),
        out_specs=P(("groups", "docs"), None),
        check_vma=False,
    )
```

time: 103 us -> 22.4 us (0.22)
  waiting for transfers between devices: 62.2 us -> 0 us
  Pallas kernels: 0 us -> 20.9 us
  matrix products: 19.9 us -> 0 us
  between operations: 13.5 us -> 0.01 us
  local copies, waits for them, and re-layouts: 6.36 us -> 1.3 us
    all_gather x2 -> x0, waiting for transfers between devices: 62.1 us -> none  [per_device(): lax.all_gather(query_list[checkpoint], 'docs', axis=0, tiled=True)]
    pallas_call x0 -> x1, Pallas kernels: none -> 20.9 us  [per_device(): pl.pallas_call(functools.partial(kernel, outer, inner, act_cuts, grad_cut...]
    dot_general x10 -> x0, matrix products: 19.9 us -> none  [the longest x4 11.6 us: fold_features(): lax.dot_general(spread, right_proj, (((0,), (0,)), ((), ())), preferred_e...]
    unnamed x14 -> x1, local copies, waits for them, and re-layouts: 4.66 us -> 1.3 us
  transfers between devices with their start and end apart: 2 -> 0, of which waited for: 2 -> 0; matrix products, arithmetic and copies ran while one was open for 17% -> 0% of each run, Pallas kernels for 0% -> 0%
where the time goes in v1:
time: 22.4 us; the launch traced here: 22.2 us
  Pallas kernels  20.9 us (93%)
  local copies, waits for them, and re-layouts  1.3 us (6%)
    pallas_call x1, Pallas kernels, per_device(): pl.pallas_call(functools.partial(kernel, outer, inner, act_cuts, grad_cut...  20.9 us
    unnamed x1, local copies, waits for them, and re-layouts  1.3 us

profile of v1, /device:TPU:0, one launch (start us, length us, event | category | flops | bytes accessed | tf_op | source)
XLA Modules:
  0.0 22.2 jit_solution(13734105807488791393)
XLA Ops:
  0.0 20.9 %shard_map.91 = f32[16,64]{1,0:T(8,128)} custom-call(bf16[2,64,4096]{2,1,0:T(8,128)(2,1)} %qa_hbm.1, bf16[2,64,11008]{2,1,0:T(8,128)(2,1)} %qg_hbm.1, s32[1,64]{1,0:T(1,128)} %qs_hbm.1, bf16[2,128,4096]{2,1,0:T(8,128)(2,1)} %da_hbm.1, bf16[2,128,11008]{2,1,0:T(8,128)(2,1)} %dg_hbm.1, s32[1,128]{1,0:T(1,128)} %ds_hbm.1, bf16[64,4096]{1,0:T(8,128)(2,1)} %bitcast.3, ...), custom_call_target="tpu_custom_call" | custom-call | tf_op jit(solution)/shard_map/pallas_call | solution.py:270
  20.9 1.3 %copy.11 = f32[16,64]{1,0:T(8,128)} copy(f32[16,64]{1,0:T(8,128)} %shard_map.91) | data formatting | bytes 8192

commit v2 on v1

v2 whole, which is shorter than its diff:
```python
import functools

import jax
import jax.numpy as jnp
from jax import lax
from jax.experimental import pallas as pl
from jax.experimental.pallas import tpu as pltpu
from jax.sharding import PartitionSpec as P

DOCS_DEV = 16
Q_DEV = 4
MESH = pl.DeviceIdType.MESH
NT = (((1,), (1,)), ((), ()))


def cuts(extent, parts):
    units = extent // 256
    edges = [256 * (units * i // parts) for i in range(parts)] + [extent]
    return list(zip(edges[:-1], edges[1:]))


def flipped(value, mask):
    bit = 1
    while bit <= mask:
        if mask & bit:
            value = value + bit - 2 * bit * ((value // bit) % 2)
        bit *= 2
    return value


def kernel(
    outer,
    inner,
    act_cuts,
    grad_cuts,
    qa_hbm,
    qg_hbm,
    qs_hbm,
    da_hbm,
    dg_hbm,
    ds_hbm,
    wi_hbm,
    wo_hbm,
    rates_ref,
    out_ref,
    qa,
    qg,
    qs,
    da,
    dg,
    ds,
    wi,
    wo,
    q_left,
    q_right,
    d_left,
    d_right,
    outgoing,
    result,
    load_sem,
    send_sem,
    recv_sem,
    pair_sem,
):
    me = lax.axis_index("docs")
    mates = 2 * inner
    row, mate = me // mates, me % mates
    col, core = mate // 2, mate % 2
    qtok = qs.shape[1]
    tok = ds.shape[1]
    tag = Q_DEV * mates
    width = 2 * qtok

    loads = []

    def load(src, dst):
        copy = pltpu.make_async_copy(src, dst, load_sem.at[len(loads)])
        copy.start()
        loads.append(copy)
        return copy

    qs_load, ds_load = load(qs_hbm, qs), load(ds_hbm, ds)
    wi_loads, qa_loads = [], []
    for a, b in act_cuts:
        wi_loads.append(load(wi_hbm.at[:, a:b], wi.at[:, a:b]))
        qa_loads.append(load(qa_hbm.at[:, :, a:b], qa.at[:, :, a:b]))
    wo_loads, qg_loads = [], []
    for a, b in grad_cuts:
        wo_loads.append(load(wo_hbm.at[:, a:b], wo.at[:, a:b]))
        qg_loads.append(load(qg_hbm.at[:, :, a:b], qg.at[:, :, a:b]))

    rows_away = [flipped(row, i) for i in range(1, outer)]
    cols_away = [flipped(col, i) for i in range(1, inner)]
    other = 1 - core

    def at(r, c, k):
        return (r * inner + c) * 2 + k

    places = [(r, c) for c in cols_away for r in rows_away] + [(r, col) for r in rows_away]
    places += [(row, c) for c in cols_away]
    peers = [at(r, c, core) for r, c in places]
    sibling = at(row, col, other)
    barrier = pltpu.get_barrier_semaphore()
    for peer in peers + [sibling]:
        pl.semaphore_signal(barrier, inc=1, device_id={"docs": peer}, device_id_type=MESH)

    sends = []

    def send(src, dst, sem, peer):
        copy = pltpu.make_async_remote_copy(
            src_ref=src,
            dst_ref=dst,
            send_sem=send_sem.at[len(sends)],
            recv_sem=sem,
            device_id={"docs": peer},
            device_id_type=MESH,
        )
        copy.start()
        sends.append(copy)

    def arrived(block, sem):
        pltpu.make_async_remote_copy(
            src_ref=block,
            dst_ref=block,
            send_sem=send_sem.at[0],
            recv_sem=sem,
            device_id={"docs": sibling},
            device_id_type=MESH,
        ).wait_recv()

    def spread(kind, blocks):
        own = blocks.at[col, row]
        for peer in peers:
            send(own, own, recv_sem.at[kind, col, row], peer)

    def share(kind, blocks):
        send(blocks.at[core], blocks.at[core], pair_sem.at[kind], sibling)

    def project(x, w, w_loads, x_loads, ranges):
        rows = x.shape[0] * x.shape[1]
        total = None
        for i, (a, b) in enumerate(ranges):
            if w_loads is not None:
                w_loads[i].wait()
            x_loads[i].wait()
            part = lax.dot_general(
                x[:, :, a:b].reshape(rows, b - a), w[:, a:b], NT, preferred_element_type=jnp.float32
            )
            total = part if total is None else total + part
        return total

    def beside(total):
        half = total.shape[0] // 2
        return jnp.concatenate([total[:half], total[half:]], axis=1).astype(jnp.bfloat16)

    qs_load.wait()
    doubled = jnp.concatenate([qs[...], qs[...]], axis=1)
    lane = lax.broadcasted_iota(jnp.int32, (tag, width), 1)
    line = lax.broadcasted_iota(jnp.int32, (tag, width), 0)
    mine = (line == doubled + mate * Q_DEV) & (lane // qtok == row % 2)
    q_left[col, row, qtok:, :] = mine.astype(jnp.float32).astype(jnp.bfloat16)
    q_left[col, row, :qtok, :] = beside(project(qa, wi, wi_loads, qa_loads, act_cuts))
    da_loads = [load(da_hbm.at[:, :, a:b], da.at[:, :, a:b]) for a, b in act_cuts]
    pl.semaphore_wait(barrier, len(peers) + 1)
    spread(0, q_left)
    half = project(qg, wo, wo_loads[:2], qg_loads[:2], grad_cuts[:2])
    dg_loads = [load(dg_hbm.at[:, :, a:b], dg.at[:, :, a:b]) for a, b in grad_cuts]
    q_right[col, row] = beside(half + project(qg, wo, wo_loads[2:], qg_loads[2:], grad_cuts[2:]))
    spread(1, q_right)

    ds_load.wait()
    of_doc = lax.broadcasted_iota(jnp.int32, (DOCS_DEV, tok), 0) == ds[...]
    d_left[core, tok:, :] = of_doc.astype(jnp.float32).astype(jnp.bfloat16)
    d_left[core, :tok, :] = beside(project(da, wi, None, da_loads, act_cuts))
    share(0, d_left)
    d_right[core] = beside(project(dg, wo, None, dg_loads, grad_cuts))
    share(1, d_right)

    def apart(block):
        lanes = lax.broadcasted_iota(jnp.int32, block.shape, 1)
        wide = block.astype(jnp.float32)
        first = lanes < block.shape[1] // 2
        both = [jnp.where(first, wide, 0.0), jnp.where(first, 0.0, wide)]
        return jnp.concatenate(both, axis=0).astype(jnp.bfloat16)

    def halves(x):
        high = x.astype(jnp.bfloat16)
        return [high, (x - high.astype(jnp.float32)).astype(jnp.bfloat16)]

    blank = jnp.zeros((tag, width), jnp.bfloat16)

    def scores(k, c):
        blocks = q_left[c]
        left = blocks[:, :qtok].reshape(outer * qtok, -1)
        right = q_right[c].reshape(outer * qtok, -1)
        of_query = jnp.concatenate(
            [
                jnp.concatenate(
                    [blocks[r, qtok:] if r // 2 == i else blank for i in range(outer // 2)], axis=1
                )
                for r in range(outer)
            ],
            axis=0,
        )
        a = lax.dot_general(apart(d_left[k, :tok]), left, NT, preferred_element_type=jnp.float32)
        b = lax.dot_general(apart(d_right[k]), right, NT, preferred_element_type=jnp.float32)
        ab = a * b
        s = ab[:tok] * rates_ref[0] + ab[tok:] * rates_ref[1]
        of = d_left[k, tok:]
        t = jnp.dot(
            jnp.concatenate([of, of], axis=1),
            jnp.concatenate(halves(s), axis=0),
            preferred_element_type=jnp.float32,
        )
        both = lax.dot_general(
            jnp.concatenate(halves(t), axis=0), of_query, NT, preferred_element_type=jnp.float32
        )
        return both[:DOCS_DEV] + both[DOCS_DEV:]

    total = theirs = None
    for c in [col] + cols_away:
        for r in [row] + rows_away if c is not col else rows_away:
            arrived(q_left.at[c, r], recv_sem.at[0, c, r])
            arrived(q_right.at[c, r], recv_sem.at[1, c, r])
        if theirs is None:
            arrived(d_left.at[other], pair_sem.at[0])
            arrived(d_right.at[other], pair_sem.at[1])
        part = scores(other, c)
        theirs = part if theirs is None else theirs + part
        if c is ([col] + cols_away)[-1]:
            outgoing[:, : theirs.shape[1]] = theirs
            send(outgoing, result, pair_sem.at[2], sibling)
        part = scores(core, c)
        total = part if total is None else total + part
    arrived(result, pair_sem.at[2])
    k = wi.shape[0]
    out_ref[...] = (total + result[:, : total.shape[1]]) * (4.0 / (k * k))

    for copy in sends:
        copy.wait_send()


def per_device(
    doc_acts,
    doc_grads,
    doc_segments,
    query_acts,
    query_grads,
    query_segments,
    input_proj,
    output_proj,
    step_rates,
):
    n = lax.axis_size("docs")
    mates = 2
    while mates * mates < n and n % (2 * mates) == 0:
        mates *= 2
    outer, inner = n // mates, mates // 2
    d, k = input_proj.shape
    f = output_proj.shape[0]
    qtok, tok = query_segments.shape[1], doc_segments.shape[1]
    act_cuts, grad_cuts = cuts(d, 2), cuts(f, 4)
    n_loads = 2 + 3 * len(act_cuts) + 3 * len(grad_cuts)
    n_sends = 2 * (outer * inner - 1) + 3
    wide = max(128, Q_DEV * n)
    hbm = pl.BlockSpec(memory_space=pl.ANY)
    return pl.pallas_call(
        functools.partial(kernel, outer, inner, act_cuts, grad_cuts),
        out_shape=jax.ShapeDtypeStruct((DOCS_DEV, Q_DEV * n), jnp.float32),
        in_specs=[hbm] * 8 + [pl.BlockSpec(memory_space=pltpu.SMEM)],
        out_specs=pl.BlockSpec(memory_space=pltpu.VMEM),
        scratch_shapes=[
            pltpu.VMEM(query_acts.shape, jnp.bfloat16),
            pltpu.VMEM(query_grads.shape, jnp.bfloat16),
            pltpu.VMEM(query_segments.shape, jnp.int32),
            pltpu.VMEM(doc_acts.shape, jnp.bfloat16),
            pltpu.VMEM(doc_grads.shape, jnp.bfloat16),
            pltpu.VMEM(doc_segments.shape, jnp.int32),
            pltpu.VMEM((k, d), jnp.bfloat16),
            pltpu.VMEM((k, f), jnp.bfloat16),
            pltpu.VMEM((inner, outer, qtok + Q_DEV * mates, 2 * k), jnp.bfloat16),
            pltpu.VMEM((inner, outer, qtok, 2 * k), jnp.bfloat16),
            pltpu.VMEM((2, tok + DOCS_DEV, 2 * k), jnp.bfloat16),
            pltpu.VMEM((2, tok, 2 * k), jnp.bfloat16),
            pltpu.VMEM((DOCS_DEV, wide), jnp.float32),
            pltpu.VMEM((DOCS_DEV, wide), jnp.float32),
            pltpu.SemaphoreType.DMA((n_loads,)),
            pltpu.SemaphoreType.DMA((n_sends,)),
            pltpu.SemaphoreType.DMA((2, inner, outer)),
            pltpu.SemaphoreType.DMA((3,)),
        ],
        compiler_params=pltpu.CompilerParams(
            collective_id=0, has_side_effects=True, vmem_limit_bytes=56 << 20
        ),
    )(
        query_acts,
        query_grads,
        query_segments,
        doc_acts,
        doc_grads,
        doc_segments,
        input_proj.T,
        output_proj.T,
        step_rates,
    )


def solution(mesh):
    return jax.shard_map(
        per_device,
        mesh=mesh,
        in_specs=(
            P(None, ("groups", "docs"), None),
            P(None, ("groups", "docs"), None),
            P(("groups", "docs"), None),
            P(None, ("groups", "docs"), None),
            P(None, ("groups", "docs"), None),
            P(("groups", "docs"), None),
            P(),
            P(),
            P(),
        ),
        out_specs=P(("groups", "docs"), None),
        check_vma=False,
    )
```

time: 22.4 us -> 19 us (0.85)
  Pallas kernels: 20.9 us -> 17.5 us
    pallas_call x1, Pallas kernels: 20.9 us -> 17.5 us  [per_device(): pl.pallas_call(functools.partial(kernel, outer, inner, act_cuts, grad_cut...]
where the time goes in v2:
time: 19 us; the launch traced here: 18.8 us
  Pallas kernels  17.5 us (92%)
  local copies, waits for them, and re-layouts  1.3 us (7%)
    pallas_call x1, Pallas kernels, per_device(): pl.pallas_call(functools.partial(kernel, outer, inner, act_cuts, grad_cut...  17.5 us
    unnamed x1, local copies, waits for them, and re-layouts  1.3 us

profile of v2, /device:TPU:0, one launch (start us, length us, event | category | flops | bytes accessed | tf_op | source)
XLA Modules:
  0.0 18.8 jit_solution(4325577450440148444)
XLA Ops:
  0.0 17.5 %shard_map.91 = f32[16,64]{1,0:T(8,128)} custom-call(bf16[2,64,4096]{2,1,0:T(8,128)(2,1)} %qa_hbm.1, bf16[2,64,11008]{2,1,0:T(8,128)(2,1)} %qg_hbm.1, s32[1,64]{1,0:T(1,128)} %qs_hbm.1, bf16[2,128,4096]{2,1,0:T(8,128)(2,1)} %da_hbm.1, bf16[2,128,11008]{2,1,0:T(8,128)(2,1)} %dg_hbm.1, s32[1,128]{1,0:T(1,128)} %ds_hbm.1, bf16[64,4096]{1,0:T(8,128)(2,1)} %bitcast.3, ...), custom_call_target="tpu_custom_call" | custom-call | tf_op jit(solution)/shard_map/pallas_call | solution.py:267
  17.5 1.3 %copy.11 = f32[16,64]{1,0:T(8,128)} copy(f32[16,64]{1,0:T(8,128)} %shard_map.91) | data formatting | bytes 8192

commit v3 on v2

--- a/solution.py
+++ b/solution.py
@@ -41,7 +41,7 @@
     ds_hbm,
     wi_hbm,
     wo_hbm,
-    rates_ref,
+    rates_hbm,
     out_ref,
     qa,
     qg,
@@ -51,6 +51,7 @@
     ds,
     wi,
     wo,
+    rates,
     q_left,
     q_right,
     d_left,
@@ -71,6 +72,21 @@
     tag = Q_DEV * mates
     width = 2 * qtok
 
+    rows_away = [flipped(row, i) for i in range(1, outer)]
+    cols_away = [flipped(col, i) for i in range(1, inner)]
+    other = 1 - core
+
+    def at(r, c, k):
+        return (r * inner + c) * 2 + k
+
+    places = [(r, c) for c in cols_away for r in rows_away] + [(r, col) for r in rows_away]
+    places += [(row, c) for c in cols_away]
+    peers = [at(r, c, core) for r, c in places]
+    sibling = at(row, col, other)
+    barrier = pltpu.get_barrier_semaphore()
+    for peer in peers + [sibling]:
+        pl.semaphore_signal(barrier, inc=1, device_id={"docs": peer}, device_id_type=MESH)
+
     loads = []
 
     def load(src, dst):
@@ -80,6 +96,7 @@
         return copy
 
     qs_load, ds_load = load(qs_hbm, qs), load(ds_hbm, ds)
+    rates_load = load(rates_hbm, rates)
     wi_loads, qa_loads = [], []
     for a, b in act_cuts:
         wi_loads.append(load(wi_hbm.at[:, a:b], wi.at[:, a:b]))
@@ -88,21 +105,6 @@
     for a, b in grad_cuts:
         wo_loads.append(load(wo_hbm.at[:, a:b], wo.at[:, a:b]))
         qg_loads.append(load(qg_hbm.at[:, :, a:b], qg.at[:, :, a:b]))
-
-    rows_away = [flipped(row, i) for i in range(1, outer)]
-    cols_away = [flipped(col, i) for i in range(1, inner)]
-    other = 1 - core
-
-    def at(r, c, k):
-        return (r * inner + c) * 2 + k
-
-    places = [(r, c) for c in cols_away for r in rows_away] + [(r, col) for r in rows_away]
-    places += [(row, c) for c in cols_away]
-    peers = [at(r, c, core) for r, c in places]
-    sibling = at(row, col, other)
-    barrier = pltpu.get_barrier_semaphore()
-    for peer in peers + [sibling]:
-        pl.semaphore_signal(barrier, inc=1, device_id={"docs": peer}, device_id_type=MESH)
 
     sends = []
 
@@ -128,10 +130,17 @@
             device_id_type=MESH,
         ).wait_recv()
 
-    def spread(kind, blocks):
+    def spread(kind, blocks, away):
         own = blocks.at[col, row]
-        for peer in peers:
-            send(own, own, recv_sem.at[kind, col, row], peer)
+        for r, c in away:
+            send(own, own, recv_sem.at[kind, col, row], at(r, c, core))
+
+    def relay(kind, blocks):
+        for r in rows_away:
+            block = blocks.at[col, r]
+            arrived(block, recv_sem.at[kind, col, r])
+            for c in cols_away:
+                send(block, block, recv_sem.at[kind, col, r], at(row, c, core))
 
     def share(kind, blocks):
         send(blocks.at[core], blocks.at[core], pair_sem.at[kind], sibling)
@@ -162,18 +171,21 @@
     q_left[col, row, :qtok, :] = beside(project(qa, wi, wi_loads, qa_loads, act_cuts))
     da_loads = [load(da_hbm.at[:, :, a:b], da.at[:, :, a:b]) for a, b in act_cuts]
     pl.semaphore_wait(barrier, len(peers) + 1)
-    spread(0, q_left)
+    spread(0, q_left, places[len(cols_away) * len(rows_away) :])
     half = project(qg, wo, wo_loads[:2], qg_loads[:2], grad_cuts[:2])
     dg_loads = [load(dg_hbm.at[:, :, a:b], dg.at[:, :, a:b]) for a, b in grad_cuts]
     q_right[col, row] = beside(half + project(qg, wo, wo_loads[2:], qg_loads[2:], grad_cuts[2:]))
-    spread(1, q_right)
+    spread(1, q_right, places)
 
     ds_load.wait()
+    rates_load.wait()
     of_doc = lax.broadcasted_iota(jnp.int32, (DOCS_DEV, tok), 0) == ds[...]
     d_left[core, tok:, :] = of_doc.astype(jnp.float32).astype(jnp.bfloat16)
     d_left[core, :tok, :] = beside(project(da, wi, None, da_loads, act_cuts))
     share(0, d_left)
-    d_right[core] = beside(project(dg, wo, None, dg_loads, grad_cuts))
+    half = project(dg, wo, None, dg_loads[:2], grad_cuts[:2])
+    relay(0, q_left)
+    d_right[core] = beside(half + project(dg, wo, None, dg_loads[2:], grad_cuts[2:]))
     share(1, d_right)
 
     def apart(block):
@@ -205,7 +217,7 @@
         a = lax.dot_general(apart(d_left[k, :tok]), left, NT, preferred_element_type=jnp.float32)
         b = lax.dot_general(apart(d_right[k]), right, NT, preferred_element_type=jnp.float32)
         ab = a * b
-        s = ab[:tok] * rates_ref[0] + ab[tok:] * rates_ref[1]
+        s = ab[:tok] * rates[0] + ab[tok:] * rates[1]
         of = d_left[k, tok:]
         t = jnp.dot(
             jnp.concatenate([of, of], axis=1),
@@ -220,18 +232,21 @@
     total = theirs = None
     for c in [col] + cols_away:
         for r in [row] + rows_away if c is not col else rows_away:
-            arrived(q_left.at[c, r], recv_sem.at[0, c, r])
+            if c is not col:
+                arrived(q_left.at[c, r], recv_sem.at[0, c, r])
             arrived(q_right.at[c, r], recv_sem.at[1, c, r])
-        if theirs is None:
+        if total is None:
+            total = scores(core, c)
             arrived(d_left.at[other], pair_sem.at[0])
             arrived(d_right.at[other], pair_sem.at[1])
-        part = scores(other, c)
-        theirs = part if theirs is None else theirs + part
+            theirs = scores(other, c)
+        else:
+            theirs = theirs + scores(other, c)
         if c is ([col] + cols_away)[-1]:
             outgoing[:, : theirs.shape[1]] = theirs
             send(outgoing, result, pair_sem.at[2], sibling)
-        part = scores(core, c)
-        total = part if total is None else total + part
+        if c is not col:
+            total = total + scores(core, c)
     arrived(result, pair_sem.at[2])
     k = wi.shape[0]
     out_ref[...] = (total + result[:, : total.shape[1]]) * (4.0 / (k * k))
@@ -259,15 +274,15 @@
     d, k = input_proj.shape
     f = output_proj.shape[0]
     qtok, tok = query_segments.shape[1], doc_segments.shape[1]
-    act_cuts, grad_cuts = cuts(d, 2), cuts(f, 4)
-    n_loads = 2 + 3 * len(act_cuts) + 3 * len(grad_cuts)
+    act_cuts, grad_cuts = cuts(d, 1), cuts(f, 4)
+    n_loads = 3 + 3 * len(act_cuts) + 3 * len(grad_cuts)
     n_sends = 2 * (outer * inner - 1) + 3
     wide = max(128, Q_DEV * n)
     hbm = pl.BlockSpec(memory_space=pl.ANY)
     return pl.pallas_call(
         functools.partial(kernel, outer, inner, act_cuts, grad_cuts),
         out_shape=jax.ShapeDtypeStruct((DOCS_DEV, Q_DEV * n), jnp.float32),
-        in_specs=[hbm] * 8 + [pl.BlockSpec(memory_space=pltpu.SMEM)],
+        in_specs=[hbm] * 9,
         out_specs=pl.BlockSpec(memory_space=pltpu.VMEM),
         scratch_shapes=[
             pltpu.VMEM(query_acts.shape, jnp.bfloat16),
@@ -278,6 +293,7 @@
             pltpu.VMEM(doc_segments.shape, jnp.int32),
             pltpu.VMEM((k, d), jnp.bfloat16),
             pltpu.VMEM((k, f), jnp.bfloat16),
+            pltpu.SMEM(step_rates.shape, jnp.float32),
             pltpu.VMEM((inner, outer, qtok + Q_DEV * mates, 2 * k), jnp.bfloat16),
             pltpu.VMEM((inner, outer, qtok, 2 * k), jnp.bfloat16),
             pltpu.VMEM((2, tok + DOCS_DEV, 2 * k), jnp.bfloat16),

time: 19 us -> 17.5 us (0.921)
  Pallas kernels: 17.5 us -> 16 us
    pallas_call x1, Pallas kernels: 17.5 us -> 16 us  [per_device(): pl.pallas_call(functools.partial(kernel, outer, inner, act_cuts, grad_cut...]
where the time goes in v3:
time: 17.5 us; the launch traced here: 17.3 us
  Pallas kernels  16 us (91%)
  local copies, waits for them, and re-layouts  1.3 us (7%)
    pallas_call x1, Pallas kernels, per_device(): pl.pallas_call(functools.partial(kernel, outer, inner, act_cuts, grad_cut...  16 us
    unnamed x1, local copies, waits for them, and re-layouts  1.3 us

profile of v3, /device:TPU:0, one launch (start us, length us, event | category | flops | bytes accessed | tf_op | source)
XLA Modules:
  0.0 17.3 jit_solution(12302496125222963756)
XLA Ops:
  0.0 16.0 %shard_map.91 = f32[16,64]{1,0:T(8,128)} custom-call(bf16[2,64,4096]{2,1,0:T(8,128)(2,1)} %qa_hbm.1, bf16[2,64,11008]{2,1,0:T(8,128)(2,1)} %qg_hbm.1, s32[1,64]{1,0:T(1,128)} %qs_hbm.1, bf16[2,128,4096]{2,1,0:T(8,128)(2,1)} %da_hbm.1, bf16[2,128,11008]{2,1,0:T(8,128)(2,1)} %dg_hbm.1, s32[1,128]{1,0:T(1,128)} %ds_hbm.1, bf16[64,4096]{1,0:T(8,128)(2,1)} %bitcast.3, ...), custom_call_target="tpu_custom_call" | custom-call | tf_op jit(solution)/shard_map/pallas_call | solution.py:282
  16.0 1.3 %copy.11 = f32[16,64]{1,0:T(8,128)} copy(f32[16,64]{1,0:T(8,128)} %shard_map.91) | data formatting | bytes 8192

commit v4 on v3

--- a/solution.py
+++ b/solution.py
@@ -172,9 +172,9 @@
     da_loads = [load(da_hbm.at[:, :, a:b], da.at[:, :, a:b]) for a, b in act_cuts]
     pl.semaphore_wait(barrier, len(peers) + 1)
     spread(0, q_left, places[len(cols_away) * len(rows_away) :])
-    half = project(qg, wo, wo_loads[:2], qg_loads[:2], grad_cuts[:2])
+    half = project(qg, wo, wo_loads[:1], qg_loads[:1], grad_cuts[:1])
     dg_loads = [load(dg_hbm.at[:, :, a:b], dg.at[:, :, a:b]) for a, b in grad_cuts]
-    q_right[col, row] = beside(half + project(qg, wo, wo_loads[2:], qg_loads[2:], grad_cuts[2:]))
+    q_right[col, row] = beside(half + project(qg, wo, wo_loads[1:], qg_loads[1:], grad_cuts[1:]))
     spread(1, q_right, places)
 
     ds_load.wait()
@@ -183,9 +183,9 @@
     d_left[core, tok:, :] = of_doc.astype(jnp.float32).astype(jnp.bfloat16)
     d_left[core, :tok, :] = beside(project(da, wi, None, da_loads, act_cuts))
     share(0, d_left)
-    half = project(dg, wo, None, dg_loads[:2], grad_cuts[:2])
+    half = project(dg, wo, None, dg_loads[:1], grad_cuts[:1])
     relay(0, q_left)
-    d_right[core] = beside(half + project(dg, wo, None, dg_loads[2:], grad_cuts[2:]))
+    d_right[core] = beside(half + project(dg, wo, None, dg_loads[1:], grad_cuts[1:]))
     share(1, d_right)
 
     def apart(block):
@@ -274,7 +274,7 @@
     d, k = input_proj.shape
     f = output_proj.shape[0]
     qtok, tok = query_segments.shape[1], doc_segments.shape[1]
-    act_cuts, grad_cuts = cuts(d, 1), cuts(f, 4)
+    act_cuts, grad_cuts = cuts(d, 1), cuts(f, 2)
     n_loads = 3 + 3 * len(act_cuts) + 3 * len(grad_cuts)
     n_sends = 2 * (outer * inner - 1) + 3
     wide = max(128, Q_DEV * n)

time: 17.5 us -> 17.1 us (0.977)
  Pallas kernels: 16 us -> 15.6 us
    pallas_call x1, Pallas kernels: 16 us -> 15.6 us  [per_device(): pl.pallas_call(functools.partial(kernel, outer, inner, act_cuts, grad_cut...]
where the time goes in v4:
time: 17.1 us; the launch traced here: 16.9 us
  Pallas kernels  15.6 us (91%)
  local copies, waits for them, and re-layouts  1.3 us (8%)
    pallas_call x1, Pallas kernels, per_device(): pl.pallas_call(functools.partial(kernel, outer, inner, act_cuts, grad_cut...  15.6 us
    unnamed x1, local copies, waits for them, and re-layouts  1.3 us

profile of v4, /device:TPU:0, one launch (start us, length us, event | category | flops | bytes accessed | tf_op | source)
XLA Modules:
  0.0 16.9 jit_solution(10687775140770515018)
XLA Ops:
  0.0 15.6 %shard_map.91 = f32[16,64]{1,0:T(8,128)} custom-call(bf16[2,64,4096]{2,1,0:T(8,128)(2,1)} %qa_hbm.1, bf16[2,64,11008]{2,1,0:T(8,128)(2,1)} %qg_hbm.1, s32[1,64]{1,0:T(1,128)} %qs_hbm.1, bf16[2,128,4096]{2,1,0:T(8,128)(2,1)} %da_hbm.1, bf16[2,128,11008]{2,1,0:T(8,128)(2,1)} %dg_hbm.1, s32[1,128]{1,0:T(1,128)} %ds_hbm.1, bf16[64,4096]{1,0:T(8,128)(2,1)} %bitcast.3, ...), custom_call_target="tpu_custom_call" | custom-call | tf_op jit(solution)/shard_map/pallas_call | solution.py:282
  15.6 1.3 %copy.11 = f32[16,64]{1,0:T(8,128)} copy(f32[16,64]{1,0:T(8,128)} %shard_map.91) | data formatting | bytes 8192
